TPU v7x, 32 devices: a whole 2x2x4 slice. The times are simulated.
32 devices in a mesh: row: 4 (over y, x), col: 8 (over z, core).
Axes of the slice: x: 2, y: 2, z: 4, core: 2. Of those that a mesh axis runs over, the one named last changes fastest.
Arguments:
- embeddings: bfloat16 [128, 256, 256], P('col'), may hold values from -0.375 to 0.375
- projection: bfloat16 [256, 64], replicated, may hold values from -4.1875 to 4.1875
- weight: bfloat16 [16384, 32768], P('row', 'col'), may hold values from -0.046875 to 0.046875
- act_grad: bfloat16 [128, 32768], P('row', 'col'), may hold values from -6 to 6
Outputs:
- activation: bfloat16 [128, 32768], P('row', 'col')
- weight_grad: float32 [16384, 32768], P('row', 'col')
- feature_grad: float32 [128, 16384], P('col', 'row')
All inputs are finite; a program needn't handle non-finite values.
Results may differ from a plain program's by a relative error of at most 0.0066.
Values may be sent and summed in bfloat16 or wider, within the bound.
A program may use at most 192 MiB of HBM per device.

v0:
```python
import jax
import jax.numpy as jnp
from jax import lax
from jax.sharding import PartitionSpec as P


def silu_slope(values):
    sig = jax.nn.sigmoid(values)
    return sig * (1.0 + values * (1.0 - sig))


def shards(embeddings, projection, weight, act_grad):
    emb_rows = weight.shape[0] // projection.shape[1]
    emb_first = lax.axis_index("row") * emb_rows
    mine_emb = lax.dynamic_slice_in_dim(embeddings, emb_first, emb_rows, 1)
    interaction = jnp.einsum(
        "bid,bmd->bim", mine_emb, embeddings, preferred_element_type=jnp.float32
    ).astype(jnp.bfloat16)
    local_features = jnp.einsum(
        "bim,mr->bir", interaction, projection, preferred_element_type=jnp.float32
    )
    local_features = local_features.astype(jnp.bfloat16).reshape(embeddings.shape[0], -1)
    features_all = lax.all_gather(local_features, "col", axis=0, tiled=True)
    block = features_all
    preact = lax.psum_scatter(
        jnp.dot(block, weight, preferred_element_type=jnp.float32),
        "row",
        scatter_dimension=0,
        tiled=True,
    )
    activation = jax.nn.silu(preact).astype(jnp.bfloat16)
    slope_mine = (act_grad.astype(jnp.float32) * silu_slope(preact)).astype(jnp.bfloat16)
    slope_all = lax.all_gather(slope_mine, "row", axis=0, tiled=True)
    weight_grad = lax.dot_general(
        features_all, slope_all, (((0,), (0,)), ((), ())), preferred_element_type=jnp.float32
    )
    block = slope_all
    feature_grad = lax.psum_scatter(
        lax.dot_general(
            block, weight, (((1,), (1,)), ((), ())), preferred_element_type=jnp.float32
        ),
        "col",
        scatter_dimension=0,
        tiled=True,
    )
    return (activation, weight_grad, feature_grad)


def solution(mesh):
    return jax.shard_map(
        shards,
        mesh=mesh,
        in_specs=(P("col", None, None), P(), P("row", "col"), P("row", "col")),
        out_specs=(P("row", "col"), P("row", "col"), P("col", "row")),
        check_vma=False,
    )
```

profile of v0, /device:TPU:0, one launch (start us, length us, event | category | flops | bytes accessed | tf_op | source)
XLA Modules:
  0.0 177.1 jit_solution(11146893868577525076)
XLA Ops:
  7.2 0.0 copy-start
  7.2 0.0 all-gather.3.cloned.1.call-start
  7.2 1.5 copy-done
  8.8 1.6 fusion.1
  10.4 0.9 reshape.9
  11.3 0.0 all-gather.3.cloned.1.call-update
  11.4 0.0 reduce-scatter.3.cloned.1.call-start
  11.4 24.9 %all-gather.3.cloned.1.call-done = bf16[128,4096]{1,0:T(8,128)(2,1)} async-done(((bf16[16,4096]{1,0:T(8,128)(2,1)}), bf16[128,4096]{1,0:T(8,128)(2,1)}) %all-gather.3.cloned.1.call-update) | async-done | bytes 1048592 | tf_op jit(solution)/shard_map/all_gather | solution.py:23
  36.3 16.7 %fusion.7 = f32[128,4096]{1,0:T(8,128)} fusion(bf16[128,4096]{1,0:T(8,128)(2,1)} %all-gather.3.cloned.1.call-done, bf16[4096,4096]{1,0:T(8,128)(2,1)} %param.6), kind=kOutput, calls=%fused_computation.9 | convolution fusion | flops 4294967296 | bytes 36700160 | tf_op jit(solution)/shard_map/dot_general | solution.py:26
  53.0 0.0 copy-start.2
  53.0 0.0 reduce-scatter.3.cloned.1.call-update
  53.1 0.0 all-gather.5.cloned.1.call-start
  53.1 34.9 %reduce-scatter.3.cloned.1.call-done = f32[32,4096]{1,0:T(8,128)} async-done(((f32[128,4096]{1,0:T(8,128)}), f32[32,4096]{1,0:T(8,128)}) %reduce-scatter.3.cloned.1.call-update) | async-done | bytes 524304 | tf_op jit(solution)/shard_map/reduce_scatter | solution.py:25
  88.0 0.0 copy-done.2
  88.1 2.1 %multiply_convert_fusion = (bf16[32,4096]{1,0:T(8,128)(2,1)}, bf16[32,4096]{1,0:T(8,128)(2,1)}) fusion(f32[32,4096]{1,0:T(8,128)} %reduce-scatter.3.cloned.1.call-done, bf16[32,4096]{1,0:T(8,128)(2,1)S(1)} %copy-done.2), kind=kLoop, calls=%fused_computation.3 | loop fusion | flops 1572864 | bytes 1310720 | tf_op jit(solution)/shard_map/convert_element_type | solution.py:32
  90.1 0.0 all-gather.5.cloned.1.call-update
  90.1 0.0 reduce-scatter.5.cloned.1.call-start
  90.2 27.1 %all-gather.5.cloned.1.call-done = bf16[128,4096]{1,0:T(8,128)(2,1)} async-done(((bf16[32,4096]{1,0:T(8,128)(2,1)}), bf16[128,4096]{1,0:T(8,128)(2,1)}) %all-gather.5.cloned.1.call-update) | async-done | bytes 1048592 | tf_op jit(solution)/shard_map/all_gather | solution.py:33
  117.3 17.3 %fusion.9 = f32[128,4096]{1,0:T(8,128)} fusion(bf16[128,4096]{1,0:T(8,128)(2,1)} %all-gather.5.cloned.1.call-done, bf16[4096,4096]{1,0:T(8,128)(2,1)} %param.6), kind=kOutput, calls=%fused_computation.11 | convolution fusion | flops 4294967296 | bytes 36700160 | tf_op jit(solution)/shard_map/dot_general | solution.py:39
  134.6 0.0 copy-start.1
  134.6 0.0 reduce-scatter.5.cloned.1.call-update
  134.6 1.2 copy-done.1
  135.8 25.4 %fusion.8 = f32[4096,4096]{1,0:T(8,128)} fusion(bf16[128,4096]{1,0:T(8,128)(2,1)S(1)} %copy-done.1, bf16[128,4096]{1,0:T(8,128)(2,1)} %all-gather.5.cloned.1.call-done), kind=kOutput, calls=%fused_computation.10 | convolution fusion | flops 4294967296 | bytes 69206016 | tf_op jit(solution)/shard_map/dot_general | solution.py:34
  161.1 9.4 %reduce-scatter.5.cloned.1.call-done = f32[16,4096]{1,0:T(8,128)} async-done(((f32[128,4096]{1,0:T(8,128)}), f32[16,4096]{1,0:T(8,128)}) %reduce-scatter.5.cloned.1.call-update) | async-done | bytes 262160 | tf_op jit(solution)/shard_map/reduce_scatter | solution.py:38
Async XLA Ops:
  7.2 1.6 copy-start
  7.2 29.1 %all-gather.3.cloned.1.call-start = ((), (), s32[]{:S(2)}) async-start(), calls=%async_computation.2 | async-start | bytes 1179648 | tf_op jit(solution)/shard_map/all_gather | solution.py:23
  11.4 76.7 %reduce-scatter.3.cloned.1.call-start = ((), (), s32[]{:S(2)}) async-start(), calls=%async_computation.3 | async-start | bytes 2621440 | tf_op jit(solution)/shard_map/reduce_scatter | solution.py:25
  53.0 35.0 %copy-start.2 = (bf16[32,4096]{1,0:T(8,128)(2,1)S(1)}, bf16[32,4096]{1,0:T(8,128)(2,1)}, u32[]{:S(2)}) copy-start(bf16[32,4096]{1,0:T(8,128)(2,1)} %param.7) | copy-start | bytes 786436
  53.1 64.2 %all-gather.5.cloned.1.call-start = ((), (), s32[]{:S(2)}) async-start(), calls=%async_computation.4 | async-start | bytes 1310720 | tf_op jit(solution)/shard_map/all_gather | solution.py:33
  90.1 80.4 %reduce-scatter.5.cloned.1.call-start = ((), (), s32[]{:S(2)}) async-start(), calls=%async_computation.5 | async-start | bytes 2359296 | tf_op jit(solution)/shard_map/reduce_scatter | solution.py:38
  134.6 1.2 copy-start.1
Sparse Core Ops, SparseCore 0:
  11.5 24.7 all-gather.2
  53.2 34.8 reduce-scatter.2
  90.6 26.6 all-gather.4
  134.7 35.8 reduce-scatter.4
where the time goes:
time: 177 us
  waiting for transfers between devices  96.4 us (54%)
  matrix products  61 us (34%)
  between operations  13.8 us (8%)
  local copies, waits for them, and re-layouts  3.68 us (2%)
  other arithmetic  2.06 us (1%)
    reduce_scatter x1, waiting for transfers between devices, shards(): lax.psum_scatter(jnp.dot(block, weight, preferred_element_type=jnp.float3...  34.9 us
    all_gather x1, waiting for transfers between devices, shards(): slope_all = lax.all_gather(slope_mine, 'row', axis=0, tiled=True)  27.1 us
    dot_general x1, matrix products, shards(): lax.dot_general(features_all, slope_all, (((0,), (0,)), ((), ())), prefer...  25.4 us
    all_gather x1, waiting for transfers between devices, shards(): features_all = lax.all_gather(local_features, 'col', axis=0, tiled=True)  24.9 us
    dot_general x1, matrix products, shards(): lax.dot_general(block, weight, (((1,), (1,)), ((), ())), preferred_elemen...  17.3 us
    dot_general x1, matrix products, shards(): jnp.dot(block, weight, preferred_element_type=jnp.float32)  16.7 us
    reduce_scatter x1, waiting for transfers between devices, shards(): lax.psum_scatter(lax.dot_general(block, weight, (((1,), (1,)), ((), ())),...  9.41 us
  transfers between devices with their start and end apart: 4, of which 4 were waited for; matrix products, arithmetic and copies ran while one was open for 14% of the time, Pallas kernels for 0%

commit v1 on v0

v1 whole, which is shorter than its diff:
```python
import functools

import jax
import jax.numpy as jnp
from jax import lax
from jax.experimental import pallas as pl
from jax.experimental.pallas import tpu as pltpu
from jax.sharding import PartitionSpec as P

MESH = pl.DeviceIdType.MESH
F32 = jnp.float32
BF16 = jnp.bfloat16


def silu_slope(values, sig):
    return sig * (1.0 + values * (1.0 - sig))


def rows_at(index, size):
    return pl.ds(pl.multiple_of(index * size, size), size)


def exchange_kernel(
    n_row,
    n_col,
    chunk,
    group,
    depth_tile,
    feat_ref,
    weight_ref,
    grad_ref,
    *refs,
):
    n_chip = n_col // 2
    act_out, feat_out, slope_out, own_out = refs[:4]
    part_outs = refs[4 : 4 + n_chip - 1]
    (
        weight,
        feats,
        slopes,
        partial,
        partial_send,
        partial_recv,
        act,
        fgrad,
        sib_send,
        sib_recv,
        own,
        parts,
        weight_sem,
        out_sem,
        part_sem,
        gather_send,
        gather_recv,
        forward_send,
        forward_recv,
        reduce_send,
        reduce_recv,
        slope_send,
        slope_recv,
        sib_send_sem,
        sib_recv_sem,
    ) = refs[4 + n_chip - 1 :]

    me_row = lax.axis_index("row")
    me_col = lax.axis_index("col")
    core = lax.rem(me_col, 2)
    chip = lax.div(me_col, 2)
    sibling = chip * 2 + (1 - core)
    mine = feat_ref.shape[0]
    kept = grad_ref.shape[0]
    depth, width = weight_ref.shape
    n_chunks = width // chunk

    def chip_at(step):
        return lax.rem(chip + step, n_chip)

    def chip_back(step):
        return lax.rem(chip + n_chip - step, n_chip)

    def row_at(step):
        return lax.rem(me_row + step, n_row)

    def cols(j):
        return pl.ds(j * chunk, chunk)

    loads = []
    for j in range(n_chunks):
        load = pltpu.make_async_copy(
            weight_ref.at[:, cols(j)], weight.at[:, cols(j)], weight_sem.at[j]
        )
        load.start()
        loads.append(load)

    barrier = pltpu.get_barrier_semaphore()
    for step in range(1, n_chip):
        pl.semaphore_signal(
            barrier, inc=1, device_id=(me_row, chip_at(step) * 2 + core), device_id_type=MESH
        )
    pl.semaphore_signal(barrier, inc=1, device_id=(me_row, sibling), device_id_type=MESH)
    for step in range(1, n_row):
        pl.semaphore_signal(barrier, inc=1, device_id=(row_at(step), me_col), device_id_type=MESH)
    pl.semaphore_wait(barrier, n_chip + n_row - 1)

    sends = []
    gathers = []
    for step in range(1, n_chip):
        copy = pltpu.make_async_remote_copy(
            src_ref=feat_ref,
            dst_ref=feats.at[rows_at(me_col, mine)],
            send_sem=gather_send.at[step],
            recv_sem=gather_recv.at[step],
            device_id=(me_row, chip_at(step) * 2 + core),
            device_id_type=MESH,
        )
        copy.start()
        gathers.append(copy)
        sends.append(copy)
    forwards = []
    for step in range(n_chip):
        block = rows_at(chip_back(step) * 2 + core, mine)
        if step > 0:
            gathers[step - 1].wait_recv()
        copy = pltpu.make_async_remote_copy(
            src_ref=feat_ref if step == 0 else feats.at[block],
            dst_ref=feats.at[block],
            send_sem=forward_send.at[step],
            recv_sem=forward_recv.at[step],
            device_id=(me_row, sibling),
            device_id_type=MESH,
        )
        copy.start()
        forwards.append(copy)
        sends.append(copy)
        if step == 0:
            feats[rows_at(me_col, mine), :] = feat_ref[...]
    for copy in forwards:
        copy.wait_recv()
    outs = [pltpu.make_async_copy(feats, feat_out, out_sem.at[0])]
    outs[0].start()

    reduces = {}
    spreads = {}

    def multiply(j):
        loads[j].wait()

        @pl.loop(0, chunk // 256)
        def _(t):
            at = pl.ds(pl.multiple_of(j * chunk + t * 256, 256), 256)
            total = jnp.dot(feats[...], weight[:, at], preferred_element_type=F32)
            partial[:, at] = total
            partial_send[:, at] = total.astype(BF16)

        reduces[j] = []
        for step in range(1, n_row):
            copy = pltpu.make_async_remote_copy(
                src_ref=partial_send.at[rows_at(row_at(step), kept), cols(j)],
                dst_ref=partial_recv.at[step - 1, :, cols(j)],
                send_sem=reduce_send.at[step - 1, j],
                recv_sem=reduce_recv.at[step - 1, j],
                device_id=(row_at(step), me_col),
                device_id_type=MESH,
            )
            copy.start()
            reduces[j].append(copy)
            sends.append(copy)

    def activate(j):
        for copy in reduces[j]:
            copy.wait_recv()
        preact = partial[rows_at(me_row, kept), cols(j)]
        for step in range(1, n_row):
            preact = preact + partial_recv[step - 1, :, cols(j)].astype(F32)
        sig = 1.0 / (1.0 + jnp.exp(-preact))
        slope = grad_ref[:, cols(j)].astype(F32) * silu_slope(preact, sig)
        slopes[rows_at(me_row, kept), cols(j)] = slope.astype(BF16)
        spreads[j] = []
        for step in range(1, n_row):
            block = slopes.at[rows_at(me_row, kept), cols(j)]
            copy = pltpu.make_async_remote_copy(
                src_ref=block,
                dst_ref=block,
                send_sem=slope_send.at[step - 1, j],
                recv_sem=slope_recv.at[step - 1, j],
                device_id=(row_at(step), me_col),
                device_id_type=MESH,
            )
            copy.start()
            spreads[j].append(copy)
            sends.append(copy)
        act[:, cols(j)] = (preact * sig).astype(BF16)

    def back(g):
        for j in range(g * group, (g + 1) * group):
            for copy in spreads[j]:
                copy.wait_recv()
        units = pl.ds(g * group * chunk, group * chunk)

        @pl.loop(0, depth // depth_tile)
        def _(t):
            at = pl.ds(pl.multiple_of(t * depth_tile, depth_tile), depth_tile)
            term = lax.dot_general(
                slopes[:, units],
                weight[at, units],
                (((1,), (1,)), ((), ())),
                preferred_element_type=F32,
            )
            if g == 0:
                fgrad[:, at] = term
            else:
                fgrad[:, at] += term

    for j in range(n_chunks):
        multiply(j)
        if j >= 2:
            activate(j - 2)
    if n_chunks > 1:
        activate(n_chunks - 2)
    n_groups = n_chunks // group
    if n_groups > 1:
        back(0)
    activate(n_chunks - 1)
    outs.append(pltpu.make_async_copy(act, act_out, out_sem.at[1]))
    outs[-1].start()
    for g in range(min(1, n_groups - 1), n_groups):
        back(g)
    outs.append(pltpu.make_async_copy(slopes, slope_out, out_sem.at[2]))
    outs[-1].start()

    swaps = []
    for step in range(n_chip):
        theirs = chip_at(step) * 2 + (1 - core)
        sib_send[step] = fgrad[rows_at(theirs, mine), :].astype(BF16)
        copy = pltpu.make_async_remote_copy(
            src_ref=sib_send.at[step],
            dst_ref=sib_recv.at[step],
            send_sem=sib_send_sem.at[step],
            recv_sem=sib_recv_sem.at[step],
            device_id=(me_row, sibling),
            device_id_type=MESH,
        )
        copy.start()
        swaps.append(copy)
        sends.append(copy)
    for step in range(n_chip):
        swaps[step].wait_recv()
        total = fgrad[rows_at(chip_at(step) * 2 + core, mine), :] + sib_recv[step].astype(F32)
        if step == 0:
            own[...] = total
            outs.append(pltpu.make_async_copy(own, own_out, out_sem.at[3]))
        else:
            parts[step - 1] = total.astype(BF16)
            outs.append(
                pltpu.make_async_copy(
                    parts.at[step - 1], part_outs[step - 1], part_sem.at[step - 1]
                )
            )
        outs[-1].start()
    for copy in sends:
        copy.wait_send()
    for copy in outs:
        copy.wait()


def exchange(mesh, features, weight, act_grad):
    n_row, n_col = mesh.shape["row"], mesh.shape["col"]
    n_chip = n_col // 2
    mine, depth = features.shape
    kept, width = act_grad.shape
    examples = mine * n_col
    chunk = width // 8 if width >= 4096 else width
    n_chunks = width // chunk
    group = min(2, n_chunks)
    depth_tile = min(512, depth)
    anywhere = pl.BlockSpec(memory_space=pl.ANY)
    vmem = pl.BlockSpec(memory_space=pltpu.VMEM)
    flops = 4 * examples * depth * width
    dma = pltpu.SemaphoreType.DMA
    return pl.pallas_call(
        functools.partial(exchange_kernel, n_row, n_col, chunk, group, depth_tile),
        out_shape=[
            jax.ShapeDtypeStruct((kept, width), BF16),
            jax.ShapeDtypeStruct((examples, depth), BF16),
            jax.ShapeDtypeStruct((examples, width), BF16),
            jax.ShapeDtypeStruct((mine, depth), F32),
        ]
        + [jax.ShapeDtypeStruct((mine, depth), BF16)] * (n_chip - 1),
        in_specs=[vmem, anywhere, vmem],
        out_specs=[anywhere] * (4 + n_chip - 1),
        scratch_shapes=[
            pltpu.VMEM((depth, width), BF16),
            pltpu.VMEM((examples, depth), BF16),
            pltpu.VMEM((examples, width), BF16),
            pltpu.VMEM((examples, width), F32),
            pltpu.VMEM((examples, width), BF16),
            pltpu.VMEM((n_row - 1, kept, width), BF16),
            pltpu.VMEM((kept, width), BF16),
            pltpu.VMEM((examples, depth), F32),
            pltpu.VMEM((n_chip, mine, depth), BF16),
            pltpu.VMEM((n_chip, mine, depth), BF16),
            pltpu.VMEM((mine, depth), F32),
            pltpu.VMEM((n_chip - 1, mine, depth), BF16),
            dma((n_chunks,)),
            dma((4,)),
            dma((n_chip - 1,)),
            dma((n_chip,)),
            dma((n_chip,)),
            dma((n_chip,)),
            dma((n_chip,)),
            dma((n_row - 1, n_chunks)),
            dma((n_row - 1, n_chunks)),
            dma((n_row - 1, n_chunks)),
            dma((n_row - 1, n_chunks)),
            dma((n_chip,)),
            dma((n_chip,)),
        ],
        compiler_params=pltpu.CompilerParams(
            collective_id=0, has_side_effects=True, vmem_limit_bytes=56 * 1024 * 1024
        ),
        cost_estimate=pl.CostEstimate(
            flops=flops, bytes_accessed=2 * depth * width, transcendentals=kept * width
        ),
    )(features, weight, act_grad)


def outer_kernel(feat_ref, slope_ref, out_ref):
    out_ref[...] = lax.dot_general(
        feat_ref[...], slope_ref[...], (((0,), (0,)), ((), ())), preferred_element_type=F32
    )


def outer(features, slopes):
    examples, depth = features.shape
    width = slopes.shape[1]
    tile = min(256, depth)
    return pl.pallas_call(
        outer_kernel,
        grid=(depth // tile,),
        out_shape=jax.ShapeDtypeStruct((depth, width), F32),
        in_specs=[
            pl.BlockSpec((examples, tile), lambda i: (0, i)),
            pl.BlockSpec((examples, width), lambda i: (0, 0)),
        ],
        out_specs=pl.BlockSpec((tile, width), lambda i: (i, 0)),
        compiler_params=pltpu.CompilerParams(vmem_limit_bytes=32 * 1024 * 1024),
        cost_estimate=pl.CostEstimate(
            flops=2 * examples * depth * width,
            bytes_accessed=4 * depth * width,
            transcendentals=0,
        ),
    )(features, slopes)


def shards(mesh, embeddings, projection, weight, act_grad):
    n_chip = mesh.shape["col"] // 2
    emb_rows = weight.shape[0] // projection.shape[1]
    emb_first = lax.axis_index("row") * emb_rows
    mine_emb = lax.dynamic_slice_in_dim(embeddings, emb_first, emb_rows, 1)
    gram = jnp.einsum(
        "bid,bmd->bim", mine_emb, embeddings, preferred_element_type=F32
    ).astype(BF16)
    features = jnp.einsum("bim,mr->bir", gram, projection, preferred_element_type=F32)
    features = features.astype(BF16).reshape(embeddings.shape[0], -1)
    activation, features_all, slopes_all, own, *parts = exchange(
        mesh, features, weight, act_grad
    )
    arrived = []
    for step in range(1, n_chip):
        pairs = [
            (2 * z + core, 2 * ((z + step) % n_chip) + core)
            for z in range(n_chip)
            for core in range(2)
        ]
        arrived.append(lax.ppermute(parts[step - 1], "col", pairs))
    weight_grad = outer(features_all, slopes_all)
    feature_grad = own
    for block in arrived:
        feature_grad = feature_grad + block.astype(F32)
    return activation, weight_grad, feature_grad


def solution(mesh):
    return jax.shard_map(
        functools.partial(shards, mesh),
        mesh=mesh,
        in_specs=(P("col", None, None), P(), P("row", "col"), P("row", "col")),
        out_specs=(P("row", "col"), P("row", "col"), P("col", "row")),
        check_vma=False,
    )
```

time: 177 us -> 93.5 us (0.53)
  waiting for transfers between devices: 96.4 us -> 0.01 us
  Pallas kernels: 0 us -> 79.5 us
  matrix products: 61 us -> 1.65 us
  between operations: 13.8 us -> 0.68 us
  starting transfers between devices: 0.16 us -> 4.89 us
  local copies, waits for them, and re-layouts: 3.68 us -> 5.68 us
    pallas_call x0 -> x2, Pallas kernels: none -> 79.5 us  [the longest x1 56.1 us: exchange(): pl.pallas_call(functools.partial(exchange_kernel, n_row, n_col, chunk, gr...]
    dot_general x4 -> x1, matrix products: 61 us -> 1.65 us  [shards(): jnp.einsum('bim,mr->bir', gram, projection, preferred_element_type=F32)]
    all_gather x2 -> x0, waiting for transfers between devices: 52 us -> none  [the longest x1 27.1 us: shards(): slope_all = lax.all_gather(slope_mine, 'row', axis=0, tiled=True)]
    reduce_scatter x2 -> x0, waiting for transfers between devices: 44.4 us -> none  [the longest x1 34.9 us: shards(): lax.psum_scatter(jnp.dot(block, weight, preferred_element_type=jnp.float3...]
    ppermute x0 -> x3, starting transfers between devices: none -> 4.89 us  [shards(): arrived.append(lax.ppermute(parts[step - 1], 'col', pairs))]
    convert_element_type x1 -> x0, other arithmetic: 2.06 us -> none  [shards(): (act_grad.astype(jnp.float32) * silu_slope(preact)).astype(jnp.bfloat16)]
    unnamed x6 -> x11, local copies, waits for them, and re-layouts: 2.74 us -> 4.74 us
  transfers between devices with their start and end apart: 4 -> 3, of which waited for: 4 -> 0; matrix products, arithmetic and copies ran while one was open for 14% -> 0% of each run, Pallas kernels for 0% -> 25%
where the time goes in v1:
time: 93.5 us; the launch traced here: 93.2 us
  Pallas kernels  79.5 us (85%)
  local copies, waits for them, and re-layouts  5.68 us (6%)
  starting transfers between devices  4.89 us (5%)
  matrix products  1.65 us (2%)
    pallas_call x1, Pallas kernels, exchange(): pl.pallas_call(functools.partial(exchange_kernel, n_row, n_col, chunk, gr...  56.1 us
    pallas_call x1, Pallas kernels, outer(): pl.pallas_call(outer_kernel, grid=(depth // tile,), out_shape=jax.ShapeDt...  23.4 us
    ppermute x3, starting transfers between devices, shards(): arrived.append(lax.ppermute(parts[step - 1], 'col', pairs))  4.89 us
    unnamed x11, local copies, waits for them, and re-layouts  4.74 us
  transfers between devices with their start and end apart: 3, of which 0 were waited for; matrix products, arithmetic and copies ran while one was open for 0% of the time, Pallas kernels for 25%

profile of v1, /device:TPU:0, one launch (start us, length us, event | category | flops | bytes accessed | tf_op | source)
XLA Modules:
  0.0 93.2 jit_solution(3824492937165048255)
XLA Ops:
  0.6 0.0 copy-start
  0.6 1.6 %copy-done = bf16[16,256,256]{2,1,0:T(8,128)(2,1)S(1)} copy-done((bf16[16,256,256]{2,1,0:T(8,128)(2,1)S(1)}, bf16[16,256,256]{2,1,0:T(8,128)(2,1)}, u32[]{:S(2)}) %copy-start) | copy-done | bytes 2097176
  2.2 1.7 %fusion.1 = bf16[16,64,64]{2,1,0:T(8,128)(2,1)S(1)} fusion(bf16[16,256,256]{2,1,0:T(8,128)(2,1)S(1)} %copy-done, s32[]{:T(128)S(6)} %select_n.3, bf16[256,64]{0,1:T(8,128)(2,1)} %param.5), kind=kOutput, calls=%fused_computation.2 | convolution fusion | flops 168099840 | bytes 2785284 | tf_op jit(solution)/shard_map/bim,mr->bir/dot_general | solution.py:363
  3.9 0.9 %reshape.9.feat_ref = bf16[16,4096]{1,0:T(8,128)(2,1)} reshape(bf16[16,64,64]{2,1,0:T(8,128)(2,1)S(1)} %fusion.1) | data formatting | bytes 262144 | tf_op jit(solution)/shard_map/reshape | solution.py:364
  4.8 56.1 %shard_map.67 = (bf16[32,4096]{1,0:T(8,128)(2,1)}, bf16[128,4096]{1,0:T(8,128)(2,1)}, bf16[128,4096]{1,0:T(8,128)(2,1)}, f32[16,4096]{1,0:T(8,128)}, bf16[16,409...) custom-call(bf16[16,4096]{1,0:T(8,128)(2,1)} %reshape.9.feat_ref, ...), custom_call_target="tpu_custom_call" | custom-call | flops 8589934592 | bytes 33554432 | tf_op jit(solution)/shard_map/pallas_call | solution.py:280
  60.9 2.1 %collective-permute-start = (bf16[16,4096]{1,0:T(8,128)(2,1)}, bf16[16,4096]{1,0:T(8,128)(2,1)S(1)}, u32[]{:S(2)}, u32[]{:S(2)}) collective-permute-start(bf16[16,4096]{1,0:T(8,128)(2,1)} %get-tuple-element.14), channel_id=1, source_target_pairs={{0,2},{1,3},{2,4},{3,5},{4,6},{5,7},{6,0},{7,1},{8,10},{9,11},{10,... | collective-permute-start | bytes 393224 | tf_op jit(solution)/shard_map/ppermute | solution.py:375
  63.1 2.6 %collective-permute-start.1 = (bf16[16,4096]{1,0:T(8,128)(2,1)}, bf16[16,4096]{1,0:T(8,128)(2,1)S(1)}, u32[]{:S(2)}, u32[]{:S(2)}) collective-permute-start(bf16[16,4096]{1,0:T(8,128)(2,1)} %get-tuple-element.15), channel_id=1, source_target_pairs={{0,4},{1,5},{2,6},{3,7},{4,0},{5,1},{6,2},{7,3},{8,12},{9,13},{10,... | collective-permute-start | bytes 393224 | tf_op jit(solution)/shard_map/ppermute | solution.py:375
  65.7 0.2 collective-permute-start.2
  65.8 0.0 copy-start.1
  65.8 1.2 %copy-done.1 = bf16[128,4096]{1,0:T(8,128)(2,1)S(1)} copy-done((bf16[128,4096]{1,0:T(8,128)(2,1)S(1)}, bf16[128,4096]{1,0:T(8,128)(2,1)}, u32[]{:S(2)}) %copy-start.1) | copy-done | bytes 1048600
  67.0 0.0 copy-start.2
  67.0 1.2 %copy-done.2 = bf16[128,4096]{1,0:T(8,128)(2,1)S(1)} copy-done((bf16[128,4096]{1,0:T(8,128)(2,1)S(1)}, bf16[128,4096]{1,0:T(8,128)(2,1)}, u32[]{:S(2)}) %copy-start.2) | copy-done | bytes 1048600
  68.3 0.0 copy-start.3
  68.3 0.0 copy-start.4
  68.3 23.4 %shard_map.68 = f32[4096,4096]{1,0:T(8,128)} custom-call(bf16[128,4096]{1,0:T(8,128)(2,1)S(1)} %copy-done.1, bf16[128,4096]{1,0:T(8,128)(2,1)S(1)} %copy-done.2), custom_call_target="tpu_custom_call" | custom-call | flops 4294967296 | bytes 67108864 | tf_op jit(solution)/shard_map/pallas_call | solution.py:337
  91.7 0.0 collective-permute-done
  91.7 0.0 collective-permute-done.1
  91.7 0.0 collective-permute-done.2
  91.7 0.0 copy-done.3
  91.7 0.8 convert_add_fusion
  92.5 0.0 copy-done.4
  92.5 0.7 copy.8
Async XLA Ops:
  0.6 1.6 %copy-start = (bf16[16,256,256]{2,1,0:T(8,128)(2,1)S(1)}, bf16[16,256,256]{2,1,0:T(8,128)(2,1)}, u32[]{:S(2)}) copy-start(bf16[16,256,256]{2,1,0:T(8,128)(2,1)} %param.4) | copy-start | bytes 6291460
  60.9 30.8 %collective-permute-start = (bf16[16,4096]{1,0:T(8,128)(2,1)}, bf16[16,4096]{1,0:T(8,128)(2,1)S(1)}, u32[]{:S(2)}, u32[]{:S(2)}) collective-permute-start(bf16[16,4096]{1,0:T(8,128)(2,1)} %get-tuple-element.14), channel_id=1, source_target_pairs={{0,2},{1,3},{2,4},{3,5},{4,6},{5,7},{6,0},{7,1},{8,10},{9,11},{10,... | collective-permute-start | bytes 393224 | tf_op jit(solution)/shard_map/ppermute | solution.py:375
  63.1 28.6 %collective-permute-start.1 = (bf16[16,4096]{1,0:T(8,128)(2,1)}, bf16[16,4096]{1,0:T(8,128)(2,1)S(1)}, u32[]{:S(2)}, u32[]{:S(2)}) collective-permute-start(bf16[16,4096]{1,0:T(8,128)(2,1)} %get-tuple-element.15), channel_id=1, source_target_pairs={{0,4},{1,5},{2,6},{3,7},{4,0},{5,1},{6,2},{7,3},{8,12},{9,13},{10,... | collective-permute-start | bytes 393224 | tf_op jit(solution)/shard_map/ppermute | solution.py:375
  65.7 26.0 %collective-permute-start.2 = (bf16[16,4096]{1,0:T(8,128)(2,1)}, bf16[16,4096]{1,0:T(8,128)(2,1)S(1)}, u32[]{:S(2)}, u32[]{:S(2)}) collective-permute-start(bf16[16,4096]{1,0:T(8,128)(2,1)} %get-tuple-element.16), channel_id=1, source_target_pairs={{0,6},{1,7},{2,0},{3,1},{4,2},{5,3},{6,4},{7,5},{8,14},{9,15},{10,... | collective-permute-start | bytes 393224 | tf_op jit(solution)/shard_map/ppermute | solution.py:375
  65.8 1.2 %copy-start.1 = (bf16[128,4096]{1,0:T(8,128)(2,1)S(1)}, bf16[128,4096]{1,0:T(8,128)(2,1)}, u32[]{:S(2)}) copy-start(bf16[128,4096]{1,0:T(8,128)(2,1)} %get-tuple-element.11.feat_ref) | copy-start | bytes 3145732
  67.0 1.2 %copy-start.2 = (bf16[128,4096]{1,0:T(8,128)(2,1)S(1)}, bf16[128,4096]{1,0:T(8,128)(2,1)}, u32[]{:S(2)}) copy-start(bf16[128,4096]{1,0:T(8,128)(2,1)} %get-tuple-element.12.slope_ref) | copy-start | bytes 3145732
  68.3 23.4 %copy-start.3 = (f32[16,4096]{1,0:T(8,128)S(1)}, f32[16,4096]{1,0:T(8,128)}, u32[]{:S(2)}) copy-start(f32[16,4096]{1,0:T(8,128)} %get-tuple-element.13) | copy-start | bytes 786436
  68.3 24.2 %copy-start.4 = (bf16[32,4096]{1,0:T(8,128)(2,1)S(1)}, bf16[32,4096]{1,0:T(8,128)(2,1)}, u32[]{:S(2)}) copy-start(bf16[32,4096]{1,0:T(8,128)(2,1)} %get-tuple-element.20) | copy-start | bytes 786436

commit v2 on v1

--- a/solution.py
+++ b/solution.py
@@ -24,7 +24,8 @@
     n_row,
     n_col,
     chunk,
-    group,
+    pieces,
+    groups,
     depth_tile,
     feat_ref,
     weight_ref,
@@ -42,6 +43,8 @@
         partial_send,
         partial_recv,
         act,
+        slopes_t,
+        fgrad_t,
         fgrad,
         sib_send,
         sib_recv,
@@ -84,10 +87,15 @@
     def cols(j):
         return pl.ds(j * chunk, chunk)
 
+    piece = depth // pieces
+
+    def span(p):
+        return pl.ds(p * piece, piece)
+
     loads = []
-    for j in range(n_chunks):
+    for p in range(pieces):
         load = pltpu.make_async_copy(
-            weight_ref.at[:, cols(j)], weight.at[:, cols(j)], weight_sem.at[j]
+            weight_ref.at[span(p), :], weight.at[span(p), :], weight_sem.at[p]
         )
         load.start()
         loads.append(load)
@@ -103,55 +111,72 @@
     pl.semaphore_wait(barrier, n_chip + n_row - 1)
 
     sends = []
-    gathers = []
-    for step in range(1, n_chip):
+    gathers = {}
+    for p in range(pieces):
+        for step in range(1, n_chip):
+            copy = pltpu.make_async_remote_copy(
+                src_ref=feat_ref.at[:, span(p)],
+                dst_ref=feats.at[rows_at(me_col, mine), span(p)],
+                send_sem=gather_send.at[step, p],
+                recv_sem=gather_recv.at[step, p],
+                device_id=(me_row, chip_at(step) * 2 + core),
+                device_id_type=MESH,
+            )
+            copy.start()
+            gathers[p, step] = copy
+            sends.append(copy)
+    feats[rows_at(me_col, mine), :] = feat_ref[...]
+    forwards = {}
+
+    def forward(p, step):
+        block = feats.at[rows_at(chip_back(step) * 2 + core, mine), span(p)]
+        if step > 0:
+            gathers[p, step].wait_recv()
         copy = pltpu.make_async_remote_copy(
-            src_ref=feat_ref,
-            dst_ref=feats.at[rows_at(me_col, mine)],
-            send_sem=gather_send.at[step],
-            recv_sem=gather_recv.at[step],
-            device_id=(me_row, chip_at(step) * 2 + core),
-            device_id_type=MESH,
-        )
-        copy.start()
-        gathers.append(copy)
-        sends.append(copy)
-    forwards = []
-    for step in range(n_chip):
-        block = rows_at(chip_back(step) * 2 + core, mine)
-        if step > 0:
-            gathers[step - 1].wait_recv()
-        copy = pltpu.make_async_remote_copy(
-            src_ref=feat_ref if step == 0 else feats.at[block],
-            dst_ref=feats.at[block],
-            send_sem=forward_send.at[step],
-            recv_sem=forward_recv.at[step],
+            src_ref=feat_ref.at[:, span(p)] if step == 0 else block,
+            dst_ref=block,
+            send_sem=forward_send.at[step, p],
+            recv_sem=forward_recv.at[step, p],
             device_id=(me_row, sibling),
             device_id_type=MESH,
         )
         copy.start()
-        forwards.append(copy)
+        forwards[p, step] = copy
         sends.append(copy)
-        if step == 0:
-            feats[rows_at(me_col, mine), :] = feat_ref[...]
-    for copy in forwards:
-        copy.wait_recv()
-    outs = [pltpu.make_async_copy(feats, feat_out, out_sem.at[0])]
+
+    for p in range(pieces):
+        forward(p, 0)
+    for step in range(1, n_chip):
+        forward(0, step)
+
+    def multiply_part(p, first, count):
+        @pl.loop(0, count // 256)
+        def _(t):
+            at = pl.ds(pl.multiple_of(first + t * 256, 256), 256)
+            term = jnp.dot(feats[:, span(p)], weight[span(p), at], preferred_element_type=F32)
+            total = term if p == 0 else partial[:, at] + term
+            partial[:, at] = total
+            if p == pieces - 1:
+                partial_send[:, at] = total.astype(BF16)
+
+    outs = []
+    for p in range(pieces):
+        for step in range(n_chip):
+            forwards[p, step].wait_recv()
+        loads[p].wait()
+        if p < pieces - 1:
+            multiply_part(p, 0, width // 2)
+            for step in range(1, n_chip):
+                forward(p + 1, step)
+            multiply_part(p, width // 2, width // 2)
+    outs.append(pltpu.make_async_copy(feats, feat_out, out_sem.at[0]))
     outs[0].start()
 
     reduces = {}
     spreads = {}
 
     def multiply(j):
-        loads[j].wait()
-
-        @pl.loop(0, chunk // 256)
-        def _(t):
-            at = pl.ds(pl.multiple_of(j * chunk + t * 256, 256), 256)
-            total = jnp.dot(feats[...], weight[:, at], preferred_element_type=F32)
-            partial[:, at] = total
-            partial_send[:, at] = total.astype(BF16)
-
+        multiply_part(pieces - 1, j * chunk, chunk)
         reduces[j] = []
         for step in range(1, n_row):
             copy = pltpu.make_async_remote_copy(
@@ -191,25 +216,28 @@
             sends.append(copy)
         act[:, cols(j)] = (preact * sig).astype(BF16)
 
-    def back(g):
-        for j in range(g * group, (g + 1) * group):
+    def arrive(g):
+        first, last = groups[g]
+        for j in range(first, last):
             for copy in spreads[j]:
                 copy.wait_recv()
-        units = pl.ds(g * group * chunk, group * chunk)
-
-        @pl.loop(0, depth // depth_tile)
+            slopes_t[cols(j), :] = slopes[:, cols(j)].T
+
+    def back(g, part, n_parts):
+        first, last = groups[g]
+        units = pl.ds(first * chunk, (last - first) * chunk)
+        base = part * (depth // n_parts)
+
+        @pl.loop(0, depth // n_parts // depth_tile)
         def _(t):
-            at = pl.ds(pl.multiple_of(t * depth_tile, depth_tile), depth_tile)
-            term = lax.dot_general(
-                slopes[:, units],
-                weight[at, units],
-                (((1,), (1,)), ((), ())),
-                preferred_element_type=F32,
-            )
-            if g == 0:
-                fgrad[:, at] = term
+            at = pl.ds(pl.multiple_of(base + t * depth_tile, depth_tile), depth_tile)
+            total = jnp.dot(weight[at, units], slopes_t[units, :], preferred_element_type=F32)
+            if g > 0:
+                total = total + fgrad_t[at, :]
+            if g < len(groups) - 1:
+                fgrad_t[at, :] = total
             else:
-                fgrad[:, at] += term
+                fgrad[:, at] = total.T
 
     for j in range(n_chunks):
         multiply(j)
@@ -217,46 +245,54 @@
             activate(j - 2)
     if n_chunks > 1:
         activate(n_chunks - 2)
-    n_groups = n_chunks // group
-    if n_groups > 1:
-        back(0)
+    if len(groups) > 1:
+        arrive(0)
+        back(0, 0, 2)
     activate(n_chunks - 1)
     outs.append(pltpu.make_async_copy(act, act_out, out_sem.at[1]))
     outs[-1].start()
-    for g in range(min(1, n_groups - 1), n_groups):
-        back(g)
+    if len(groups) > 1:
+        back(0, 1, 2)
+    for g in range(1, len(groups) - 1):
+        arrive(g)
+        back(g, 0, 1)
+    arrive(len(groups) - 1)
     outs.append(pltpu.make_async_copy(slopes, slope_out, out_sem.at[2]))
     outs[-1].start()
 
     swaps = []
-    for step in range(n_chip):
-        theirs = chip_at(step) * 2 + (1 - core)
-        sib_send[step] = fgrad[rows_at(theirs, mine), :].astype(BF16)
+    for p in range(pieces):
+        back(len(groups) - 1, p, pieces)
+        for step in range(n_chip):
+            theirs = chip_at(step) * 2 + (1 - core)
+            sib_send[step, :, span(p)] = fgrad[rows_at(theirs, mine), span(p)].astype(BF16)
         copy = pltpu.make_async_remote_copy(
-            src_ref=sib_send.at[step],
-            dst_ref=sib_recv.at[step],
-            send_sem=sib_send_sem.at[step],
-            recv_sem=sib_recv_sem.at[step],
+            src_ref=sib_send.at[:, :, span(p)],
+            dst_ref=sib_recv.at[:, :, span(p)],
+            send_sem=sib_send_sem.at[p],
+            recv_sem=sib_recv_sem.at[p],
             device_id=(me_row, sibling),
             device_id_type=MESH,
         )
         copy.start()
         swaps.append(copy)
         sends.append(copy)
-    for step in range(n_chip):
-        swaps[step].wait_recv()
-        total = fgrad[rows_at(chip_at(step) * 2 + core, mine), :] + sib_recv[step].astype(F32)
-        if step == 0:
-            own[...] = total
-            outs.append(pltpu.make_async_copy(own, own_out, out_sem.at[3]))
-        else:
-            parts[step - 1] = total.astype(BF16)
-            outs.append(
-                pltpu.make_async_copy(
-                    parts.at[step - 1], part_outs[step - 1], part_sem.at[step - 1]
-                )
-            )
+    for p in range(pieces):
+        swaps[p].wait_recv()
+        for step in range(n_chip):
+            held = fgrad[rows_at(chip_at(step) * 2 + core, mine), span(p)]
+            total = held + sib_recv[step, :, span(p)].astype(F32)
+            if step == 0:
+                own[:, span(p)] = total
+            else:
+                parts[step - 1, :, span(p)] = total.astype(BF16)
+    for step in range(1, n_chip):
+        outs.append(
+            pltpu.make_async_copy(parts.at[step - 1], part_outs[step - 1], part_sem.at[step - 1])
+        )
         outs[-1].start()
+    outs.append(pltpu.make_async_copy(own, own_out, out_sem.at[3]))
+    outs[-1].start()
     for copy in sends:
         copy.wait_send()
     for copy in outs:
@@ -271,14 +307,15 @@
     examples = mine * n_col
     chunk = width // 8 if width >= 4096 else width
     n_chunks = width // chunk
-    group = min(2, n_chunks)
+    pieces = 4 if depth >= 4096 else 1
+    groups = ((0, 4), (4, 6), (6, 8)) if n_chunks == 8 else ((0, n_chunks),)
     depth_tile = min(512, depth)
     anywhere = pl.BlockSpec(memory_space=pl.ANY)
     vmem = pl.BlockSpec(memory_space=pltpu.VMEM)
     flops = 4 * examples * depth * width
     dma = pltpu.SemaphoreType.DMA
     return pl.pallas_call(
-        functools.partial(exchange_kernel, n_row, n_col, chunk, group, depth_tile),
+        functools.partial(exchange_kernel, n_row, n_col, chunk, pieces, groups, depth_tile),
         out_shape=[
             jax.ShapeDtypeStruct((kept, width), BF16),
             jax.ShapeDtypeStruct((examples, depth), BF16),
@@ -296,24 +333,26 @@
             pltpu.VMEM((examples, width), BF16),
             pltpu.VMEM((n_row - 1, kept, width), BF16),
             pltpu.VMEM((kept, width), BF16),
+            pltpu.VMEM((width, examples), BF16),
+            pltpu.VMEM((depth, examples), F32),
             pltpu.VMEM((examples, depth), F32),
             pltpu.VMEM((n_chip, mine, depth), BF16),
             pltpu.VMEM((n_chip, mine, depth), BF16),
             pltpu.VMEM((mine, depth), F32),
             pltpu.VMEM((n_chip - 1, mine, depth), BF16),
-            dma((n_chunks,)),
+            dma((pieces,)),
             dma((4,)),
             dma((n_chip - 1,)),
-            dma((n_chip,)),
-            dma((n_chip,)),
-            dma((n_chip,)),
-            dma((n_chip,)),
+            dma((n_chip, pieces)),
+            dma((n_chip, pieces)),
+            dma((n_chip, pieces)),
+            dma((n_chip, pieces)),
             dma((n_row - 1, n_chunks)),
             dma((n_row - 1, n_chunks)),
             dma((n_row - 1, n_chunks)),
             dma((n_row - 1, n_chunks)),
-            dma((n_chip,)),
-            dma((n_chip,)),
+            dma((pieces,)),
+            dma((pieces,)),
         ],
         compiler_params=pltpu.CompilerParams(
             collective_id=0, has_side_effects=True, vmem_limit_bytes=56 * 1024 * 1024
@@ -333,17 +372,17 @@
 def outer(features, slopes):
     examples, depth = features.shape
     width = slopes.shape[1]
-    tile = min(256, depth)
+    tall, wide = min(1024, depth), min(1024, width)
     return pl.pallas_call(
         outer_kernel,
-        grid=(depth // tile,),
+        grid=(depth // tall, width // wide),
         out_shape=jax.ShapeDtypeStruct((depth, width), F32),
         in_specs=[
-            pl.BlockSpec((examples, tile), lambda i: (0, i)),
-            pl.BlockSpec((examples, width), lambda i: (0, 0)),
+            pl.BlockSpec((examples, tall), lambda i, j: (0, i)),
+            pl.BlockSpec((examples, wide), lambda i, j: (0, j)),
         ],
-        out_specs=pl.BlockSpec((tile, width), lambda i: (i, 0)),
-        compiler_params=pltpu.CompilerParams(vmem_limit_bytes=32 * 1024 * 1024),
+        out_specs=pl.BlockSpec((tall, wide), lambda i, j: (i, j)),
+        compiler_params=pltpu.CompilerParams(vmem_limit_bytes=60 * 1024 * 1024),
         cost_estimate=pl.CostEstimate(
             flops=2 * examples * depth * width,
             bytes_accessed=4 * depth * width,

time: 93.5 us -> 97.6 us (1.044)
  Pallas kernels: 79.5 us -> 86.3 us
  local copies, waits for them, and re-layouts: 5.68 us -> 3.23 us
    pallas_call x2, Pallas kernels: 79.5 us -> 86.3 us  [the longest x1 61.8 us: exchange(): pl.pallas_call(functools.partial(exchange_kernel, n_row, n_col, chunk, pi...]
    unnamed x11 -> x7, local copies, waits for them, and re-layouts: 4.74 us -> 2.29 us
where the time goes in v2:
time: 97.6 us; the launch traced here: 97 us
  Pallas kernels  86.3 us (88%)
  starting transfers between devices  4.43 us (5%)
  local copies, waits for them, and re-layouts  3.23 us (3%)
  matrix products  1.65 us (2%)
    pallas_call x1, Pallas kernels, exchange(): pl.pallas_call(functools.partial(exchange_kernel, n_row, n_col, chunk, pi...  61.8 us
    pallas_call x1, Pallas kernels, outer(): pl.pallas_call(outer_kernel, grid=(depth // tall, width // wide), out_sha...  24.4 us
    ppermute x3, starting transfers between devices, shards(): arrived.append(lax.ppermute(parts[step - 1], 'col', pairs))  4.43 us
    unnamed x7, local copies, waits for them, and re-layouts  2.29 us
  transfers between devices with their start and end apart: 3, of which 0 were waited for; matrix products, arithmetic and copies ran while one was open for 0% of the time, Pallas kernels for 25%

profile of v2, /device:TPU:0, one launch (start us, length us, event | category | flops | bytes accessed | tf_op | source)
XLA Modules:
  0.0 97.0 jit_solution(4867741250803885722)
XLA Ops:
  0.6 0.0 copy-start
  0.6 1.6 %copy-done = bf16[16,256,256]{2,1,0:T(8,128)(2,1)S(1)} copy-done((bf16[16,256,256]{2,1,0:T(8,128)(2,1)S(1)}, bf16[16,256,256]{2,1,0:T(8,128)(2,1)}, u32[]{:S(2)}) %copy-start) | copy-done | bytes 2097176
  2.2 1.7 %fusion.1 = bf16[16,64,64]{2,1,0:T(8,128)(2,1)S(1)} fusion(bf16[16,256,256]{2,1,0:T(8,128)(2,1)S(1)} %copy-done, s32[]{:T(128)S(6)} %select_n.3, bf16[256,64]{0,1:T(8,128)(2,1)} %param.5), kind=kOutput, calls=%fused_computation.2 | convolution fusion | flops 168099840 | bytes 2785284 | tf_op jit(solution)/shard_map/bim,mr->bir/dot_general | solution.py:402
  3.9 0.9 reshape.9.feat_ref
  4.8 61.8 %shard_map.67 = (bf16[32,4096]{1,0:T(8,128)(2,1)}, bf16[128,4096]{1,0:T(8,128)(2,1)}, bf16[128,4096]{1,0:T(8,128)(2,1)}, f32[16,4096]{1,0:T(8,128)}, bf16[16,409...) custom-call(bf16[16,4096]{1,0:T(8,128)(2,1)} %reshape.9.feat_ref, ...), custom_call_target="tpu_custom_call" | custom-call | flops 8589934592 | bytes 33554432 | tf_op jit(solution)/shard_map/pallas_call | solution.py:317
  66.7 2.0 %collective-permute-start = (bf16[16,4096]{1,0:T(8,128)(2,1)}, bf16[16,4096]{1,0:T(8,128)(2,1)S(1)}, u32[]{:S(2)}, u32[]{:S(2)}) collective-permute-start(bf16[16,4096]{1,0:T(8,128)(2,1)} %get-tuple-element.14), channel_id=1, source_target_pairs={{0,2},{1,3},{2,4},{3,5},{4,6},{5,7},{6,0},{7,1},{8,10},{9,11},{10,... | collective-permute-start | bytes 393224 | tf_op jit(solution)/shard_map/ppermute | solution.py:414
  68.7 2.2 %collective-permute-start.1 = (bf16[16,4096]{1,0:T(8,128)(2,1)}, bf16[16,4096]{1,0:T(8,128)(2,1)S(1)}, u32[]{:S(2)}, u32[]{:S(2)}) collective-permute-start(bf16[16,4096]{1,0:T(8,128)(2,1)} %get-tuple-element.15), channel_id=1, source_target_pairs={{0,4},{1,5},{2,6},{3,7},{4,0},{5,1},{6,2},{7,3},{8,12},{9,13},{10,... | collective-permute-start | bytes 393224 | tf_op jit(solution)/shard_map/ppermute | solution.py:414
  70.9 0.2 collective-permute-start.2
  71.1 0.0 copy-start.1
  71.1 0.0 copy-start.2
  71.1 24.4 %shard_map.68 = f32[4096,4096]{1,0:T(8,128)} custom-call(bf16[128,4096]{1,0:T(8,128)(2,1)} %get-tuple-element.11.feat_ref, bf16[128,4096]{1,0:T(8,128)(2,1)} %get-tuple-element.12.slope_ref), custom_call_target="tpu_custom_call" | custom-call | flops 4294967296 | bytes 67108864 | tf_op jit(solution)/shard_map/pallas_call | solution.py:376
  95.5 0.0 collective-permute-done
  95.5 0.0 collective-permute-done.1
  95.6 0.0 collective-permute-done.2
  95.6 0.0 copy-done.1
  95.6 0.8 convert_add_fusion
  96.3 0.0 copy-done.2
  96.3 0.7 copy.8
Async XLA Ops:
  0.6 1.6 %copy-start = (bf16[16,256,256]{2,1,0:T(8,128)(2,1)S(1)}, bf16[16,256,256]{2,1,0:T(8,128)(2,1)}, u32[]{:S(2)}) copy-start(bf16[16,256,256]{2,1,0:T(8,128)(2,1)} %param.4) | copy-start | bytes 6291460
  66.7 28.9 %collective-permute-start = (bf16[16,4096]{1,0:T(8,128)(2,1)}, bf16[16,4096]{1,0:T(8,128)(2,1)S(1)}, u32[]{:S(2)}, u32[]{:S(2)}) collective-permute-start(bf16[16,4096]{1,0:T(8,128)(2,1)} %get-tuple-element.14), channel_id=1, source_target_pairs={{0,2},{1,3},{2,4},{3,5},{4,6},{5,7},{6,0},{7,1},{8,10},{9,11},{10,... | collective-permute-start | bytes 393224 | tf_op jit(solution)/shard_map/ppermute | solution.py:414
  68.7 26.9 %collective-permute-start.1 = (bf16[16,4096]{1,0:T(8,128)(2,1)}, bf16[16,4096]{1,0:T(8,128)(2,1)S(1)}, u32[]{:S(2)}, u32[]{:S(2)}) collective-permute-start(bf16[16,4096]{1,0:T(8,128)(2,1)} %get-tuple-element.15), channel_id=1, source_target_pairs={{0,4},{1,5},{2,6},{3,7},{4,0},{5,1},{6,2},{7,3},{8,12},{9,13},{10,... | collective-permute-start | bytes 393224 | tf_op jit(solution)/shard_map/ppermute | solution.py:414
  70.9 24.7 %collective-permute-start.2 = (bf16[16,4096]{1,0:T(8,128)(2,1)}, bf16[16,4096]{1,0:T(8,128)(2,1)S(1)}, u32[]{:S(2)}, u32[]{:S(2)}) collective-permute-start(bf16[16,4096]{1,0:T(8,128)(2,1)} %get-tuple-element.16), channel_id=1, source_target_pairs={{0,6},{1,7},{2,0},{3,1},{4,2},{5,3},{6,4},{7,5},{8,14},{9,15},{10,... | collective-permute-start | bytes 393224 | tf_op jit(solution)/shard_map/ppermute | solution.py:414
  71.1 24.5 %copy-start.1 = (f32[16,4096]{1,0:T(8,128)S(1)}, f32[16,4096]{1,0:T(8,128)}, u32[]{:S(2)}) copy-start(f32[16,4096]{1,0:T(8,128)} %get-tuple-element.13) | copy-start | bytes 786436
  71.1 25.2 %copy-start.2 = (bf16[32,4096]{1,0:T(8,128)(2,1)S(1)}, bf16[32,4096]{1,0:T(8,128)(2,1)}, u32[]{:S(2)}) copy-start(bf16[32,4096]{1,0:T(8,128)(2,1)} %get-tuple-element.20) | copy-start | bytes 786436

commit v3 on v2

--- a/solution.py
+++ b/solution.py
@@ -93,9 +93,9 @@
         return pl.ds(p * piece, piece)
 
     loads = []
-    for p in range(pieces):
+    for j in range(n_chunks):
         load = pltpu.make_async_copy(
-            weight_ref.at[span(p), :], weight.at[span(p), :], weight_sem.at[p]
+            weight_ref.at[:, cols(j)], weight.at[:, cols(j)], weight_sem.at[j]
         )
         load.start()
         loads.append(load)
@@ -111,72 +111,50 @@
     pl.semaphore_wait(barrier, n_chip + n_row - 1)
 
     sends = []
-    gathers = {}
-    for p in range(pieces):
-        for step in range(1, n_chip):
-            copy = pltpu.make_async_remote_copy(
-                src_ref=feat_ref.at[:, span(p)],
-                dst_ref=feats.at[rows_at(me_col, mine), span(p)],
-                send_sem=gather_send.at[step, p],
-                recv_sem=gather_recv.at[step, p],
-                device_id=(me_row, chip_at(step) * 2 + core),
-                device_id_type=MESH,
-            )
-            copy.start()
-            gathers[p, step] = copy
-            sends.append(copy)
-    feats[rows_at(me_col, mine), :] = feat_ref[...]
-    forwards = {}
-
-    def forward(p, step):
-        block = feats.at[rows_at(chip_back(step) * 2 + core, mine), span(p)]
+    gathers = []
+    for step in range(1, n_chip):
+        copy = pltpu.make_async_remote_copy(
+            src_ref=feat_ref,
+            dst_ref=feats.at[rows_at(me_col, mine)],
+            send_sem=gather_send.at[step],
+            recv_sem=gather_recv.at[step],
+            device_id=(me_row, chip_at(step) * 2 + core),
+            device_id_type=MESH,
+        )
+        copy.start()
+        gathers.append(copy)
+        sends.append(copy)
+    forwards = []
+    for step in range(n_chip):
+        block = rows_at(chip_back(step) * 2 + core, mine)
         if step > 0:
-            gathers[p, step].wait_recv()
+            gathers[step - 1].wait_recv()
         copy = pltpu.make_async_remote_copy(
-            src_ref=feat_ref.at[:, span(p)] if step == 0 else block,
-            dst_ref=block,
-            send_sem=forward_send.at[step, p],
-            recv_sem=forward_recv.at[step, p],
+            src_ref=feat_ref if step == 0 else feats.at[block],
+            dst_ref=feats.at[block],
+            send_sem=forward_send.at[step],
+            recv_sem=forward_recv.at[step],
             device_id=(me_row, sibling),
             device_id_type=MESH,
         )
         copy.start()
-        forwards[p, step] = copy
+        forwards.append(copy)
         sends.append(copy)
-
-    for p in range(pieces):
-        forward(p, 0)
-    for step in range(1, n_chip):
-        forward(0, step)
-
-    def multiply_part(p, first, count):
-        @pl.loop(0, count // 256)
-        def _(t):
-            at = pl.ds(pl.multiple_of(first + t * 256, 256), 256)
-            term = jnp.dot(feats[:, span(p)], weight[span(p), at], preferred_element_type=F32)
-            total = term if p == 0 else partial[:, at] + term
-            partial[:, at] = total
-            if p == pieces - 1:
-                partial_send[:, at] = total.astype(BF16)
-
-    outs = []
-    for p in range(pieces):
-        for step in range(n_chip):
-            forwards[p, step].wait_recv()
-        loads[p].wait()
-        if p < pieces - 1:
-            multiply_part(p, 0, width // 2)
-            for step in range(1, n_chip):
-                forward(p + 1, step)
-            multiply_part(p, width // 2, width // 2)
-    outs.append(pltpu.make_async_copy(feats, feat_out, out_sem.at[0]))
+        if step == 0:
+            feats[rows_at(me_col, mine), :] = feat_ref[...]
+    for copy in forwards:
+        copy.wait_recv()
+    outs = [pltpu.make_async_copy(feats, feat_out, out_sem.at[0])]
     outs[0].start()
 
     reduces = {}
     spreads = {}
 
     def multiply(j):
-        multiply_part(pieces - 1, j * chunk, chunk)
+        loads[j].wait()
+        total = jnp.dot(feats[...], weight[:, cols(j)], preferred_element_type=F32)
+        partial[:, cols(j)] = total
+        partial_send[:, cols(j)] = total.astype(BF16)
         reduces[j] = []
         for step in range(1, n_row):
             copy = pltpu.make_async_remote_copy(
@@ -308,8 +286,8 @@
     chunk = width // 8 if width >= 4096 else width
     n_chunks = width // chunk
     pieces = 4 if depth >= 4096 else 1
-    groups = ((0, 4), (4, 6), (6, 8)) if n_chunks == 8 else ((0, n_chunks),)
-    depth_tile = min(512, depth)
+    groups = ((0, 4), (4, 8)) if n_chunks == 8 else ((0, n_chunks),)
+    depth_tile = min(1024, depth)
     anywhere = pl.BlockSpec(memory_space=pl.ANY)
     vmem = pl.BlockSpec(memory_space=pltpu.VMEM)
     flops = 4 * examples * depth * width
@@ -340,13 +318,13 @@
             pltpu.VMEM((n_chip, mine, depth), BF16),
             pltpu.VMEM((mine, depth), F32),
             pltpu.VMEM((n_chip - 1, mine, depth), BF16),
-            dma((pieces,)),
+            dma((n_chunks,)),
             dma((4,)),
             dma((n_chip - 1,)),
-            dma((n_chip, pieces)),
-            dma((n_chip, pieces)),
-            dma((n_chip, pieces)),
-            dma((n_chip, pieces)),
+            dma((n_chip,)),
+            dma((n_chip,)),
+            dma((n_chip,)),
+            dma((n_chip,)),
             dma((n_row - 1, n_chunks)),
             dma((n_row - 1, n_chunks)),
             dma((n_row - 1, n_chunks)),

time: 97.6 us -> 91.9 us (0.942)
  Pallas kernels: 86.3 us -> 80 us
    pallas_call x1, Pallas kernels: 61.8 us -> 55.5 us  [exchange(): pl.pallas_call(functools.partial(exchange_kernel, n_row, n_col, chunk, pi...]
  transfers between devices with their start and end apart: 3 -> 3, of which waited for: 0 -> 0; matrix products, arithmetic and copies ran while one was open for 0% -> 0% of each run, Pallas kernels for 25% -> 27%
where the time goes in v3:
time: 91.9 us; the launch traced here: 91.5 us
  Pallas kernels  80 us (87%)
  starting transfers between devices  5.21 us (6%)
  local copies, waits for them, and re-layouts  3.23 us (4%)
  matrix products  1.65 us (2%)
    pallas_call x1, Pallas kernels, exchange(): pl.pallas_call(functools.partial(exchange_kernel, n_row, n_col, chunk, pi...  55.5 us
    pallas_call x1, Pallas kernels, outer(): pl.pallas_call(outer_kernel, grid=(depth // tall, width // wide), out_sha...  24.4 us
    ppermute x3, starting transfers between devices, shards(): arrived.append(lax.ppermute(parts[step - 1], 'col', pairs))  5.21 us
    unnamed x7, local copies, waits for them, and re-layouts  2.29 us
  transfers between devices with their start and end apart: 3, of which 0 were waited for; matrix products, arithmetic and copies ran while one was open for 0% of the time, Pallas kernels for 27%

profile of v3, /device:TPU:0, one launch (start us, length us, event | category | flops | bytes accessed | tf_op | source)
XLA Modules:
  0.0 91.5 jit_solution(12888150443900116079)
XLA Ops:
  0.6 0.0 copy-start
  0.6 1.6 %copy-done = bf16[16,256,256]{2,1,0:T(8,128)(2,1)S(1)} copy-done((bf16[16,256,256]{2,1,0:T(8,128)(2,1)S(1)}, bf16[16,256,256]{2,1,0:T(8,128)(2,1)}, u32[]{:S(2)}) %copy-start) | copy-done | bytes 2097176
  2.2 1.6 %fusion.1 = bf16[16,64,64]{2,1,0:T(8,128)(2,1)S(1)} fusion(bf16[16,256,256]{2,1,0:T(8,128)(2,1)S(1)} %copy-done, s32[]{:T(128)S(6)} %select_n.3, bf16[256,64]{0,1:T(8,128)(2,1)} %param.5), kind=kOutput, calls=%fused_computation.2 | convolution fusion | flops 168099840 | bytes 2785284 | tf_op jit(solution)/shard_map/bim,mr->bir/dot_general | solution.py:380
  3.9 0.9 %reshape.9.feat_ref = bf16[16,4096]{1,0:T(8,128)(2,1)} reshape(bf16[16,64,64]{2,1,0:T(8,128)(2,1)S(1)} %fusion.1) | data formatting | bytes 262144 | tf_op jit(solution)/shard_map/reshape | solution.py:381
  4.8 55.5 %shard_map.67 = (bf16[32,4096]{1,0:T(8,128)(2,1)}, bf16[128,4096]{1,0:T(8,128)(2,1)}, bf16[128,4096]{1,0:T(8,128)(2,1)}, f32[16,4096]{1,0:T(8,128)}, bf16[16,409...) custom-call(bf16[16,4096]{1,0:T(8,128)(2,1)} %reshape.9.feat_ref, ...), custom_call_target="tpu_custom_call" | custom-call | flops 8589934592 | bytes 33554432 | tf_op jit(solution)/shard_map/pallas_call | solution.py:295
  60.4 2.8 %collective-permute-start = (bf16[16,4096]{1,0:T(8,128)(2,1)}, bf16[16,4096]{1,0:T(8,128)(2,1)S(1)}, u32[]{:S(2)}, u32[]{:S(2)}) collective-permute-start(bf16[16,4096]{1,0:T(8,128)(2,1)} %get-tuple-element.14), channel_id=1, source_target_pairs={{0,2},{1,3},{2,4},{3,5},{4,6},{5,7},{6,0},{7,1},{8,10},{9,11},{10,... | collective-permute-start | bytes 393224 | tf_op jit(solution)/shard_map/ppermute | solution.py:392
  63.1 2.1 %collective-permute-start.1 = (bf16[16,4096]{1,0:T(8,128)(2,1)}, bf16[16,4096]{1,0:T(8,128)(2,1)S(1)}, u32[]{:S(2)}, u32[]{:S(2)}) collective-permute-start(bf16[16,4096]{1,0:T(8,128)(2,1)} %get-tuple-element.15), channel_id=1, source_target_pairs={{0,4},{1,5},{2,6},{3,7},{4,0},{5,1},{6,2},{7,3},{8,12},{9,13},{10,... | collective-permute-start | bytes 393224 | tf_op jit(solution)/shard_map/ppermute | solution.py:392
  65.3 0.3 collective-permute-start.2
  65.6 0.0 copy-start.1
  65.6 0.0 copy-start.2
  65.6 24.4 %shard_map.68 = f32[4096,4096]{1,0:T(8,128)} custom-call(bf16[128,4096]{1,0:T(8,128)(2,1)} %get-tuple-element.11.feat_ref, bf16[128,4096]{1,0:T(8,128)(2,1)} %get-tuple-element.12.slope_ref), custom_call_target="tpu_custom_call" | custom-call | flops 4294967296 | bytes 67108864 | tf_op jit(solution)/shard_map/pallas_call | solution.py:354
  90.0 0.0 collective-permute-done
  90.0 0.0 collective-permute-done.1
  90.0 0.0 collective-permute-done.2
  90.1 0.0 copy-done.1
  90.1 0.8 convert_add_fusion
  90.8 0.0 copy-done.2
  90.8 0.7 copy.8
Async XLA Ops:
  0.6 1.6 %copy-start = (bf16[16,256,256]{2,1,0:T(8,128)(2,1)S(1)}, bf16[16,256,256]{2,1,0:T(8,128)(2,1)}, u32[]{:S(2)}) copy-start(bf16[16,256,256]{2,1,0:T(8,128)(2,1)} %param.4) | copy-start | bytes 6291460
  60.4 29.7 %collective-permute-start = (bf16[16,4096]{1,0:T(8,128)(2,1)}, bf16[16,4096]{1,0:T(8,128)(2,1)S(1)}, u32[]{:S(2)}, u32[]{:S(2)}) collective-permute-start(bf16[16,4096]{1,0:T(8,128)(2,1)} %get-tuple-element.14), channel_id=1, source_target_pairs={{0,2},{1,3},{2,4},{3,5},{4,6},{5,7},{6,0},{7,1},{8,10},{9,11},{10,... | collective-permute-start | bytes 393224 | tf_op jit(solution)/shard_map/ppermute | solution.py:392
  63.1 26.9 %collective-permute-start.1 = (bf16[16,4096]{1,0:T(8,128)(2,1)}, bf16[16,4096]{1,0:T(8,128)(2,1)S(1)}, u32[]{:S(2)}, u32[]{:S(2)}) collective-permute-start(bf16[16,4096]{1,0:T(8,128)(2,1)} %get-tuple-element.15), channel_id=1, source_target_pairs={{0,4},{1,5},{2,6},{3,7},{4,0},{5,1},{6,2},{7,3},{8,12},{9,13},{10,... | collective-permute-start | bytes 393224 | tf_op jit(solution)/shard_map/ppermute | solution.py:392
  65.3 24.8 %collective-permute-start.2 = (bf16[16,4096]{1,0:T(8,128)(2,1)}, bf16[16,4096]{1,0:T(8,128)(2,1)S(1)}, u32[]{:S(2)}, u32[]{:S(2)}) collective-permute-start(bf16[16,4096]{1,0:T(8,128)(2,1)} %get-tuple-element.16), channel_id=1, source_target_pairs={{0,6},{1,7},{2,0},{3,1},{4,2},{5,3},{6,4},{7,5},{8,14},{9,15},{10,... | collective-permute-start | bytes 393224 | tf_op jit(solution)/shard_map/ppermute | solution.py:392
  65.6 24.5 %copy-start.1 = (f32[16,4096]{1,0:T(8,128)S(1)}, f32[16,4096]{1,0:T(8,128)}, u32[]{:S(2)}) copy-start(f32[16,4096]{1,0:T(8,128)} %get-tuple-element.13) | copy-start | bytes 786436
  65.6 25.2 %copy-start.2 = (bf16[32,4096]{1,0:T(8,128)(2,1)S(1)}, bf16[32,4096]{1,0:T(8,128)(2,1)}, u32[]{:S(2)}) copy-start(bf16[32,4096]{1,0:T(8,128)(2,1)} %get-tuple-element.20) | copy-start | bytes 786436

commit v4 on v3

--- a/solution.py
+++ b/solution.py
@@ -286,7 +286,7 @@
     chunk = width // 8 if width >= 4096 else width
     n_chunks = width // chunk
     pieces = 4 if depth >= 4096 else 1
-    groups = ((0, 4), (4, 8)) if n_chunks == 8 else ((0, n_chunks),)
+    groups = ((0, 4), (4, 7), (7, 8)) if n_chunks == 8 else ((0, n_chunks),)
     depth_tile = min(1024, depth)
     anywhere = pl.BlockSpec(memory_space=pl.ANY)
     vmem = pl.BlockSpec(memory_space=pltpu.VMEM)

time: 91.9 us -> 88.4 us (0.962)
  Pallas kernels: 80 us -> 77 us
    pallas_call x1, Pallas kernels: 55.5 us -> 52.5 us  [exchange(): pl.pallas_call(functools.partial(exchange_kernel, n_row, n_col, chunk, pi...]
  transfers between devices with their start and end apart: 3 -> 3, of which waited for: 0 -> 0; matrix products, arithmetic and copies ran while one was open for 0% -> 0% of each run, Pallas kernels for 27% -> 28%
where the time goes in v4:
time: 88.4 us; the launch traced here: 88 us
  Pallas kernels  77 us (87%)
  starting transfers between devices  4.7 us (5%)
  local copies, waits for them, and re-layouts  3.23 us (4%)
  matrix products  1.65 us (2%)
    pallas_call x1, Pallas kernels, exchange(): pl.pallas_call(functools.partial(exchange_kernel, n_row, n_col, chunk, pi...  52.5 us
    pallas_call x1, Pallas kernels, outer(): pl.pallas_call(outer_kernel, grid=(depth // tall, width // wide), out_sha...  24.4 us
    ppermute x3, starting transfers between devices, shards(): arrived.append(lax.ppermute(parts[step - 1], 'col', pairs))  4.7 us
    unnamed x7, local copies, waits for them, and re-layouts  2.29 us
  transfers between devices with their start and end apart: 3, of which 0 were waited for; matrix products, arithmetic and copies ran while one was open for 0% of the time, Pallas kernels for 28%

profile of v4, /device:TPU:0, one launch (start us, length us, event | category | flops | bytes accessed | tf_op | source)
XLA Modules:
  0.0 88.0 jit_solution(16996738719666957874)
XLA Ops:
  0.6 0.0 copy-start
  0.6 1.6 %copy-done = bf16[16,256,256]{2,1,0:T(8,128)(2,1)S(1)} copy-done((bf16[16,256,256]{2,1,0:T(8,128)(2,1)S(1)}, bf16[16,256,256]{2,1,0:T(8,128)(2,1)}, u32[]{:S(2)}) %copy-start) | copy-done | bytes 2097176
  2.2 1.7 %fusion.1 = bf16[16,64,64]{2,1,0:T(8,128)(2,1)S(1)} fusion(bf16[16,256,256]{2,1,0:T(8,128)(2,1)S(1)} %copy-done, s32[]{:T(128)S(6)} %select_n.3, bf16[256,64]{0,1:T(8,128)(2,1)} %param.5), kind=kOutput, calls=%fused_computation.2 | convolution fusion | flops 168099840 | bytes 2785284 | tf_op jit(solution)/shard_map/bim,mr->bir/dot_general | solution.py:380
  3.9 0.9 %reshape.9.feat_ref = bf16[16,4096]{1,0:T(8,128)(2,1)} reshape(bf16[16,64,64]{2,1,0:T(8,128)(2,1)S(1)} %fusion.1) | data formatting | bytes 262144 | tf_op jit(solution)/shard_map/reshape | solution.py:381
  4.8 52.5 %shard_map.67 = (bf16[32,4096]{1,0:T(8,128)(2,1)}, bf16[128,4096]{1,0:T(8,128)(2,1)}, bf16[128,4096]{1,0:T(8,128)(2,1)}, f32[16,4096]{1,0:T(8,128)}, bf16[16,409...) custom-call(bf16[16,4096]{1,0:T(8,128)(2,1)} %reshape.9.feat_ref, ...), custom_call_target="tpu_custom_call" | custom-call | flops 8589934592 | bytes 33554432 | tf_op jit(solution)/shard_map/pallas_call | solution.py:295
  57.3 2.1 %collective-permute-start = (bf16[16,4096]{1,0:T(8,128)(2,1)}, bf16[16,4096]{1,0:T(8,128)(2,1)S(1)}, u32[]{:S(2)}, u32[]{:S(2)}) collective-permute-start(bf16[16,4096]{1,0:T(8,128)(2,1)} %get-tuple-element.14), channel_id=1, source_target_pairs={{0,2},{1,3},{2,4},{3,5},{4,6},{5,7},{6,0},{7,1},{8,10},{9,11},{10,... | collective-permute-start | bytes 393224 | tf_op jit(solution)/shard_map/ppermute | solution.py:392
  59.5 2.6 %collective-permute-start.1 = (bf16[16,4096]{1,0:T(8,128)(2,1)}, bf16[16,4096]{1,0:T(8,128)(2,1)S(1)}, u32[]{:S(2)}, u32[]{:S(2)}) collective-permute-start(bf16[16,4096]{1,0:T(8,128)(2,1)} %get-tuple-element.15), channel_id=1, source_target_pairs={{0,4},{1,5},{2,6},{3,7},{4,0},{5,1},{6,2},{7,3},{8,12},{9,13},{10,... | collective-permute-start | bytes 393224 | tf_op jit(solution)/shard_map/ppermute | solution.py:392
  62.0 0.0 collective-permute-start.2
  62.0 0.0 copy-start.1
  62.0 0.0 copy-start.2
  62.1 24.4 %shard_map.68 = f32[4096,4096]{1,0:T(8,128)} custom-call(bf16[128,4096]{1,0:T(8,128)(2,1)} %get-tuple-element.11.feat_ref, bf16[128,4096]{1,0:T(8,128)(2,1)} %get-tuple-element.12.slope_ref), custom_call_target="tpu_custom_call" | custom-call | flops 4294967296 | bytes 67108864 | tf_op jit(solution)/shard_map/pallas_call | solution.py:354
  86.5 0.0 collective-permute-done
  86.5 0.0 collective-permute-done.1
  86.5 0.0 collective-permute-done.2
  86.5 0.0 copy-done.1
  86.5 0.8 convert_add_fusion
  87.3 0.0 copy-done.2
  87.3 0.7 copy.8
Async XLA Ops:
  0.6 1.6 %copy-start = (bf16[16,256,256]{2,1,0:T(8,128)(2,1)S(1)}, bf16[16,256,256]{2,1,0:T(8,128)(2,1)}, u32[]{:S(2)}) copy-start(bf16[16,256,256]{2,1,0:T(8,128)(2,1)} %param.4) | copy-start | bytes 6291460
  57.3 29.2 %collective-permute-start = (bf16[16,4096]{1,0:T(8,128)(2,1)}, bf16[16,4096]{1,0:T(8,128)(2,1)S(1)}, u32[]{:S(2)}, u32[]{:S(2)}) collective-permute-start(bf16[16,4096]{1,0:T(8,128)(2,1)} %get-tuple-element.14), channel_id=1, source_target_pairs={{0,2},{1,3},{2,4},{3,5},{4,6},{5,7},{6,0},{7,1},{8,10},{9,11},{10,... | collective-permute-start | bytes 393224 | tf_op jit(solution)/shard_map/ppermute | solution.py:392
  59.5 27.1 %collective-permute-start.1 = (bf16[16,4096]{1,0:T(8,128)(2,1)}, bf16[16,4096]{1,0:T(8,128)(2,1)S(1)}, u32[]{:S(2)}, u32[]{:S(2)}) collective-permute-start(bf16[16,4096]{1,0:T(8,128)(2,1)} %get-tuple-element.15), channel_id=1, source_target_pairs={{0,4},{1,5},{2,6},{3,7},{4,0},{5,1},{6,2},{7,3},{8,12},{9,13},{10,... | collective-permute-start | bytes 393224 | tf_op jit(solution)/shard_map/ppermute | solution.py:392
  62.0 24.5 %collective-permute-start.2 = (bf16[16,4096]{1,0:T(8,128)(2,1)}, bf16[16,4096]{1,0:T(8,128)(2,1)S(1)}, u32[]{:S(2)}, u32[]{:S(2)}) collective-permute-start(bf16[16,4096]{1,0:T(8,128)(2,1)} %get-tuple-element.16), channel_id=1, source_target_pairs={{0,6},{1,7},{2,0},{3,1},{4,2},{5,3},{6,4},{7,5},{8,14},{9,15},{10,... | collective-permute-start | bytes 393224 | tf_op jit(solution)/shard_map/ppermute | solution.py:392
  62.0 24.5 %copy-start.1 = (f32[16,4096]{1,0:T(8,128)S(1)}, f32[16,4096]{1,0:T(8,128)}, u32[]{:S(2)}) copy-start(f32[16,4096]{1,0:T(8,128)} %get-tuple-element.13) | copy-start | bytes 786436
  62.0 25.2 %copy-start.2 = (bf16[32,4096]{1,0:T(8,128)(2,1)S(1)}, bf16[32,4096]{1,0:T(8,128)(2,1)}, u32[]{:S(2)}) copy-start(bf16[32,4096]{1,0:T(8,128)(2,1)} %get-tuple-element.20) | copy-start | bytes 786436
